TPU v7x, 256 devices: a whole 4x4x8 slice. The times are simulated.
256 devices in a mesh: tile: 4 (over z_hi, core), epoch: 64 (over x, z_lo, y).
Axes of the slice: x: 4, y: 4, z: 8 (z_hi: 2, z_lo: 4; z = z_hi * 4 + z_lo), core: 2. Of those that a mesh axis runs over, the one named last changes fastest.
Arguments:
- coadd_image: float32 [4, 512, 1024], P('tile', 'epoch'), may hold values from -6 to 6
- science: float32 [4, 64, 256, 256], P('tile', 'epoch'), may hold values from -6 to 14
- row_offset: int32 [4, 64], P('tile', 'epoch'), may hold values from 15 to 241
- col_offset: int32 [4, 64], P('tile', 'epoch'), may hold values from 15 to 753
- intersections: int32 [4, 64], P('tile', 'epoch'), may hold values 0 or 1
- visit_weight: float32 [4, 64], P('tile', 'epoch'), may hold values from 0.25 to 4
- basis_index: int32 [4, 64, 2, 3, 2], P('tile', 'epoch'), may hold values from 0 to 15
- weights: float32 [4, 64, 2, 2, 3], P('tile', 'epoch'), may hold values from 0.3 to 1.5
- profiles: float32 [16, 31], replicated, may hold values from -1 to 1
Outputs:
- mean_difference: float32 [4, 512, 1024], P('tile', 'epoch')
All inputs are finite; a program needn't handle non-finite values. No bound on the sum of `intersections` on one device may be relied on, other than what follows from the above.
Results may differ from a plain program's by a relative error of at most 0.0003.
Values sent between devices are 32-bit elements; how exact they have to be, the bound alone decides.
A program may use at most 64 MiB of HBM per device.

v0:
```python
import jax
import jax.numpy as jnp
from jax import lax
from jax.sharding import PartitionSpec as P

RW = 128
B = 3
NPROF = 16


def spread_columns(taps, region_width):
    regions = taps.shape[0]
    wide = jnp.broadcast_to(taps[:, None], (regions, region_width) + taps.shape[1:])
    return wide.reshape((regions * region_width,) + taps.shape[1:])


def convolve(window_in, taps_one, weight_map):
    kernel_len = taps_one.shape[-1]
    win_rows = window_in.shape[0] - kernel_len + 1
    win_cols = window_in.shape[1] - kernel_len + 1
    horizontal = spread_columns(taps_one[:, :, 0], RW)
    vertical = spread_columns(taps_one[:, :, 1], RW)
    region_rows = weight_map.shape[0]
    region_cols = weight_map.shape[1]
    result = jnp.zeros((win_rows, win_cols), jnp.float32)
    for basis_id in range(B):
        across = jnp.zeros((win_rows + kernel_len - 1, win_cols), jnp.float32)
        for offset in range(kernel_len):
            across = (
                across
                + horizontal[:, basis_id, offset][None, :]
                * window_in[:, offset : offset + win_cols]
            )
        downward = jnp.zeros((win_rows, win_cols), jnp.float32)
        for offset in range(kernel_len):
            downward = (
                downward
                + vertical[:, basis_id, offset][None, :] * across[offset : offset + win_rows, :]
            )
        scaled = (
            downward.reshape(region_rows, RW, region_cols, RW)
            * weight_map[:, None, :, None, basis_id]
        )
        result = result + scaled.reshape(win_rows, win_cols)
    return result


def on_device(
    coadd_image,
    science,
    row_offset,
    col_offset,
    intersections,
    visit_weight,
    basis_index,
    weights,
    profiles,
):
    tile_image = lax.all_gather(coadd_image, "epoch", axis=1, tiled=True)[0]
    win_rows = science.shape[2]
    win_cols = science.shape[3]
    kernel_len = profiles.shape[1]
    half_width = (kernel_len - 1) // 2
    one_hot = (basis_index[0][..., None] == jnp.arange(NPROF, dtype=jnp.int32)).astype(jnp.float32)
    tap_table = jnp.einsum("sxbcp,pk->sxbck", one_hot, profiles, precision=lax.Precision.HIGHEST)
    flags = intersections[0].astype(jnp.float32)
    gains = flags * visit_weight[0]
    slot_index = 0
    row_start = row_offset[0, slot_index] - half_width
    col_start = col_offset[0, slot_index] - half_width
    window_in = lax.dynamic_slice(
        tile_image, (row_start, col_start), (win_rows + kernel_len - 1, win_cols + kernel_len - 1)
    )
    residual = science[0, slot_index] - convolve(
        window_in, tap_table[slot_index], weights[0, slot_index]
    )
    residuals = [residual]
    slot_sums = jnp.stack([jnp.sum(member) for member in residuals]) * flags
    visit_total, visit_count = lax.psum((slot_sums, flags * float(win_rows * win_cols)), "tile")
    level = visit_total / jnp.maximum(visit_count, 1.0)
    diff_frame = jnp.zeros(tile_image.shape, jnp.float32)
    slot_index = 0
    corner = (row_offset[0, slot_index], col_offset[0, slot_index])
    difference = (residuals[slot_index] - level[slot_index]) * gains[slot_index]
    diff_frame = lax.dynamic_update_slice(diff_frame, difference, corner)
    cover_frame = jnp.zeros(tile_image.shape, jnp.float32)
    slot_index = 0
    corner = (row_offset[0, slot_index], col_offset[0, slot_index])
    region = lax.dynamic_slice(cover_frame, corner, (win_rows, win_cols))
    cover_frame = lax.dynamic_update_slice(cover_frame, region + gains[slot_index], corner)
    total_sum, coverage = (
        lax.psum_scatter(diff_frame[None], "epoch", scatter_dimension=1, tiled=True),
        lax.psum_scatter(cover_frame[None], "epoch", scatter_dimension=1, tiled=True),
    )
    return total_sum / jnp.maximum(coverage, 1.0)


def solution(mesh):
    return jax.shard_map(
        on_device,
        mesh=mesh,
        in_specs=(
            P("tile", "epoch", None),
            P("tile", "epoch", None, None),
            P("tile", "epoch"),
            P("tile", "epoch"),
            P("tile", "epoch"),
            P("tile", "epoch"),
            P("tile", "epoch", None, None, None),
            P("tile", "epoch", None, None, None),
            P(),
        ),
        out_specs=P("tile", "epoch", None),
        check_vma=False,
    )
```

profile of v0, /device:TPU:0, one launch (start us, length us, event | category | flops | bytes accessed | tf_op | source)
XLA Modules:
  0.0 1115.0 jit_solution(14344658755794950459)
XLA Ops:
  6.5 0.7 all-gather.2.cloned.1.call-update
  9.9 0.2 broadcast_in_dim.21.clone.1
  10.2 4.6 dynamic_update_slice.9
  14.8 1.3 copy-done.2
  16.2 0.2 fusion.93
  16.6 0.2 broadcast_in_dim.25
  17.0 0.2 broadcast_in_dim.23
  17.3 0.2 slice_reduce_fusion.2
  17.6 342.3 %all-gather.2.cloned.1.call-done = f32[1,512,1024]{2,1,0:T(8,128)} async-done(((f32[1,8,1024]{2,1,0:T(8,128)}), f32[1,512,1024]{2,1,0:T(8,128)}) %all-gather.2.cloned.1.call-update) | async-done | bytes 2097168 | tf_op jit(solution)/shard_map/all_gather | solution.py:59
  360.0 1.3 dynamic-slice_bitcast_fusion
  361.2 2.4 multiply_add_fusion.2
  363.6 2.4 multiply_add_fusion.1
  366.0 2.4 multiply_add_fusion
  368.4 0.1 mul.2103
  368.5 0.1 mul.2293
  368.7 0.1 mul.2483
  368.8 4.6 fusion.96
  374.1 10.6 all-reduce
  386.0 0.2 broadcast_in_dim.21.clone
  386.2 4.6 dynamic_update_slice.8
  390.8 1.3 copy-done.1
  392.1 343.4 %reduce-scatter.5.cloned.1.call-done = f32[1,8,1024]{2,1,0:T(8,128)} async-done(((f32[1,512,1024]{2,1,0:T(8,128)}), f32[1,8,1024]{2,1,0:T(8,128)}) %reduce-scatter.5.cloned.1.call-update) | async-done | bytes 32784 | tf_op jit(solution)/shard_map/reduce_scatter | solution.py:93
  735.5 371.6 %reduce-scatter.3.cloned.1.call-done = f32[1,8,1024]{2,1,0:T(8,128)} async-done(((f32[1,512,1024]{2,1,0:T(8,128)}), f32[1,8,1024]{2,1,0:T(8,128)}) %reduce-scatter.3.cloned.1.call-update) | async-done | bytes 32784 | tf_op jit(solution)/shard_map/reduce_scatter | solution.py:92
  1107.1 1.4 maximum_divide_fusion
  (32 shorter events, 0.8 us)
Async XLA Ops:
  6.5 9.7 copy-start
  6.5 353.4 %all-gather.2.cloned.1.call-start = ((), (), s32[]{:S(2)}) async-start(), calls=%async_computation.2 | async-start | bytes 2129920 | tf_op jit(solution)/shard_map/all_gather | solution.py:59
  7.3 728.3 %reduce-scatter.5.cloned.1.call-start = ((), (), s32[]{:S(2)}) async-start(), calls=%async_computation.4 | async-start | bytes 2129920 | tf_op jit(solution)/shard_map/reduce_scatter | solution.py:93
  9.9 6.3 copy-start.5
  10.2 7.1 copy-start.4
  14.8 1.3 copy-start.2
  16.1 1091.0 %reduce-scatter.3.cloned.1.call-start = ((), (), s32[]{:S(2)}) async-start(), calls=%async_computation.3 | async-start | bytes 2129920 | tf_op jit(solution)/shard_map/reduce_scatter | solution.py:92
  366.0 2.8 copy-start.3
  390.8 1.3 copy-start.1
Sparse Core Ops, SparseCore 0:
  9.1 350.7 all-gather.1
  362.5 373.0 reduce-scatter.4
  738.2 368.8 reduce-scatter.2
where the time goes:
time: 1120 us
  waiting for transfers between devices  1060 us (95%)
  between operations  17.9 us (2%)
  local copies, waits for them, and re-layouts  15 us (1%)
  other arithmetic  13.2 us (1%)
    reduce_scatter x1, waiting for transfers between devices, on_device(): lax.psum_scatter(diff_frame[None], 'epoch', scatter_dimension=1, tiled=True)  372 us
    reduce_scatter x1, waiting for transfers between devices, on_device(): lax.psum_scatter(cover_frame[None], 'epoch', scatter_dimension=1, tiled=T...  343 us
    all_gather x1, waiting for transfers between devices, on_device(): tile_image = lax.all_gather(coadd_image, 'epoch', axis=1, tiled=True)[0]  342 us
  transfers between devices with their start and end apart: 3, of which 3 were waited for; matrix products, arithmetic and copies ran while one was open for 2% of the time, Pallas kernels for 0%

commit v1 on v0

v1 whole, which is shorter than its diff:
```python
import jax
import jax.numpy as jnp
from jax import lax
from jax.experimental import pallas as pl
from jax.experimental.pallas import tpu as pltpu
from jax.sharding import PartitionSpec as P

KW = 31
HALF = 15
RW = 128
B = 3
F32 = jnp.float32
BF16 = jnp.bfloat16
MESH = pl.DeviceIdType.MESH

STRIDES = (16, 4, 1)
PARTS = (
    (0, 384, (1, 2, 0)),
    (384, 384, (1, 0, 2)),
    (768, 256, (2, 0, 1)),
)
NPART = len(PARTS)
ROWS = 512
COLS = 512


def split(value):
    high = value.astype(BF16)
    return high, (value - high.astype(F32)).astype(BF16)


def dot3(a_high, a_low, b_high, b_low):
    def dot(a, b):
        return jnp.dot(a, b, preferred_element_type=F32)

    return dot(a_high, b_high) + (dot(a_high, b_low) + dot(a_low, b_high))


def roll_by(value, amount, axis):
    chosen = jnp.broadcast_to(amount, value.shape)
    step = 1
    while step < value.shape[axis]:
        value = jnp.where((chosen & step) != 0, pltpu.roll(value, step, axis), value)
        step *= 2
    return value


def toeplitz(taps, shift, rows):
    width = taps.shape[1]
    base = roll_by(jnp.broadcast_to(taps, (8, width)), shift, 1)
    return pltpu.roll(jnp.broadcast_to(base[0:1, :], (rows, width)), 0, 1, stride=1, stride_axis=0)


def kernel(
    coadd, science, row_offset, col_offset, intersections, visit_weight, basis_index, weights, profiles,
    out,
    tile, sci, table, hor_hi, hor_lo, ver_hi, ver_lo, slots, recv, info, infos, cover, offs, levels, sums,
    local_sem, send_sem, recv_sem, info_send, info_recv, sum_send, sum_recv, a2a_sem, lev_sem,
):
    me_t = lax.axis_index("tile")
    me = lax.axis_index("epoch")
    coord = (me // 16, (me // 4) % 4, me % 4)

    own_copy = pltpu.make_async_copy(coadd.at[0], tile.at[coord[0], coord[1], coord[2]], local_sem.at[0])
    own_copy.start()
    sci_copy = pltpu.make_async_copy(science.at[0, 0], sci, local_sem.at[1])
    sci_copy.start()

    def peer(axis, k):
        here = coord[axis]
        return me + (lax.rem(here + k, 4) - here) * STRIDES[axis]

    barrier = pltpu.get_barrier_semaphore()
    for axis in range(3):
        for k in (1, 2, 3):
            pl.semaphore_signal(barrier, inc=1, device_id={"epoch": peer(axis, k)}, device_id_type=MESH)
    for k in (1, 2, 3):
        pl.semaphore_signal(barrier, inc=1, device_id={"tile": lax.rem(me_t + k, 4)}, device_id_type=MESH)

    oy = row_offset[0, 0]
    ox = col_offset[0, 0]
    flag = intersections[0, 0].astype(F32)
    gain = flag * visit_weight[0, 0]
    lane = lax.broadcasted_iota(jnp.int32, (1, 128), 1)
    info[coord[0], coord[1], coord[2]] = jnp.where(
        lane == 0, oy.astype(F32), jnp.where(lane == 1, ox.astype(F32), gain)
    )
    own_copy.wait()
    pl.semaphore_wait(barrier, 12)

    def stage_copies(buffer, cols, order, stage, sends, recvs):
        axis = order[stage]
        where = tuple(slice(None) if a in order[:stage] else coord[a] for a in range(3))
        block = buffer.at[where + ((slice(None),) if cols is None else (slice(None), pl.ds(*cols)))]
        return [
            pltpu.make_async_remote_copy(
                src_ref=block,
                dst_ref=block,
                send_sem=sends.at[k - 1],
                recv_sem=recvs.at[k - 1],
                device_id={"epoch": peer(axis, k)},
                device_id_type=MESH,
            )
            for k in (1, 2, 3)
        ]

    def part_copies(part, stage):
        lo, width, order = PARTS[part]
        return stage_copies(tile, (lo, width), order, stage, send_sem.at[part, stage], recv_sem.at[part, stage])

    def info_copies(stage):
        return stage_copies(info, None, (1, 2, 0), stage, info_send.at[stage], info_recv.at[stage])

    started = []

    def start_stage(stage):
        for part in range(NPART):
            if stage:
                for copy in part_copies(part, stage - 1):
                    copy.wait_recv()
            for copy in part_copies(part, stage):
                copy.start()
                started.append(copy)
        if stage:
            for copy in info_copies(stage - 1):
                copy.wait_recv()
        for copy in info_copies(stage):
            copy.start()
            started.append(copy)

    start_stage(0)

    row_start = oy - HALF
    col_start = ox - HALF
    col_block = jnp.minimum(col_start >> 7, (1024 - COLS) // 128)
    row_shift = row_start
    col_shift = col_start - 128 * col_block

    table[...] = jnp.zeros_like(table)
    table[:, 0:KW] = profiles[...]

    profile = lax.broadcasted_iota(jnp.int32, (16, COLS), 0)

    def taps_of(index):
        return jnp.sum(jnp.where(profile == index, table[...], 0.0), axis=0, keepdims=True)

    def make_horizontal(s):
        for b in range(B):
            taps = taps_of(basis_index[0, 0, s, b, 0])
            band = toeplitz(taps, col_shift + s * RW, RW).T
            at = (s * B + b) * RW
            hor_hi[:, at : at + RW], hor_lo[:, at : at + RW] = split(band)

    def make_vertical(s):
        for b in range(B):
            taps = taps_of(basis_index[0, 0, s, b, 1])
            band = toeplitz(taps, row_shift, 2 * RW)
            row = lax.broadcasted_iota(jnp.int32, (2 * RW, 1), 0)
            band = band * jnp.where(row < RW, weights[0, 0, 0, s, b], weights[0, 0, 1, s, b])
            ver_hi[s * B + b], ver_lo[s * B + b] = split(band)

    make_horizontal(0)
    start_stage(1)
    make_horizontal(1)
    start_stage(2)
    make_vertical(0)
    make_vertical(1)

    for copy in info_copies(2):
        copy.wait_recv()
    for e in range(64):
        infos[e : e + 1, :] = info[e // 16, (e // 4) % 4, e % 4]
    every = infos[...]
    offs[...] = jnp.broadcast_to(every[:, 0:1], (64, 128))
    column = lax.broadcasted_iota(jnp.int32, (64, 1024), 1).astype(F32)
    first = every[:, 1:2]
    cover[...] = jnp.where((column >= first) & (column < first + 256.0), 1.0, 0.0)

    sci_copy.wait()
    for part in range(NPART):
        for copy in part_copies(part, 2):
            copy.wait_recv()

    window = [tile[:, :, :, :, j * 128 : (j + 1) * 128].reshape(ROWS, 128) for j in range(8)]
    chosen = jnp.broadcast_to(col_block, (ROWS, 128))
    for step in (4, 2, 1):
        keep = COLS // 128 + step - 1
        moved = (chosen & step) != 0
        window = [
            jnp.where(moved, window[j + step], window[j]) if j + step < len(window) else window[j]
            for j in range(min(keep, len(window)))
        ]
    window = jnp.concatenate(window, axis=1)
    win_hi, win_lo = split(window)
    total = jnp.zeros((1, RW), F32)
    for s in range(2):
        across = dot3(
            win_hi, win_lo, hor_hi[:, s * B * RW : (s + 1) * B * RW], hor_lo[:, s * B * RW : (s + 1) * B * RW]
        )
        model = None
        for b in range(B):
            x_hi, x_lo = split(across[:, b * RW : (b + 1) * RW])
            term = dot3(ver_hi[s * B + b], ver_lo[s * B + b], x_hi, x_lo)
            model = term if model is None else model + term
        residual = sci[:, s * RW : (s + 1) * RW] - model
        total = total + jnp.sum(residual, axis=0, keepdims=True)
        sci[:, s * RW : (s + 1) * RW] = residual * gain
    sums[me_t] = jnp.where(
        lax.broadcasted_iota(jnp.int32, (2, RW), 0) == 0, jnp.sum(total) * flag, flag
    )

    sum_copies = [
        pltpu.make_async_remote_copy(
            src_ref=sums.at[me_t],
            dst_ref=sums.at[me_t],
            send_sem=sum_send.at[k - 1],
            recv_sem=sum_recv.at[k - 1],
            device_id={"tile": lax.rem(me_t + k, 4)},
            device_id_type=MESH,
        )
        for k in (1, 2, 3)
    ]
    for copy in sum_copies:
        copy.start()

    folded = roll_by(roll_by(sci[...], ox & 255, 1), oy & 255, 0)
    slots[...] = folded.reshape(32, 8, 256)

    def send_block(k, carry):
        target = lax.rem(me + k, 64)
        pltpu.make_async_remote_copy(
            src_ref=slots.at[lax.rem(target, 32)],
            dst_ref=recv.at[me],
            send_sem=a2a_sem.at[0],
            recv_sem=a2a_sem.at[1],
            device_id={"epoch": target},
            device_id_type=MESH,
        ).start()
        return carry

    lax.fori_loop(1, 64, send_block, 0)
    recv[me] = slots[lax.rem(me, 32)]

    for copy in sum_copies:
        copy.wait_recv()
    residual_sum = sums[0, 0:1, :] + sums[1, 0:1, :] + sums[2, 0:1, :] + sums[3, 0:1, :]
    flags = sums[0, 1:2, :] + sums[1, 1:2, :] + sums[2, 1:2, :] + sums[3, 1:2, :]
    levels[me] = gain * (residual_sum / jnp.maximum(flags * 65536.0, 1.0))

    def send_level(k, carry):
        target = lax.rem(me + k, 64)
        pltpu.make_async_remote_copy(
            src_ref=levels.at[me],
            dst_ref=levels.at[me],
            send_sem=lev_sem.at[0],
            recv_sem=lev_sem.at[1],
            device_id={"epoch": target},
            device_id_type=MESH,
        ).start()
        return carry

    lax.fori_loop(1, 64, send_level, 0)

    for copy in started:
        copy.wait_send()
    for copy in sum_copies:
        copy.wait_send()

    def wait_for(ref, sem):
        pltpu.make_async_copy(ref, ref, sem).wait()

    most = pl.ds(0, 63)
    wait_for(recv.at[most], a2a_sem.at[0])
    wait_for(levels.at[most], lev_sem.at[0])
    wait_for(recv.at[most], a2a_sem.at[1])
    wait_for(levels.at[most], lev_sem.at[1])

    my_row = (me * 8 + lax.broadcasted_iota(jnp.int32, (8, RW), 0)).astype(F32)
    out_blocks = 8

    def add_block(e, carry):
        acc, cnt = carry
        first_row = jnp.broadcast_to(offs[pl.ds(e, 1), :], (8, RW))
        held = jnp.where((my_row >= first_row) & (my_row < first_row + 256.0), 1.0, 0.0)
        level = levels[e]
        left = (recv[e, :, 0:RW] - level) * held
        right = (recv[e, :, RW : 2 * RW] - level) * held
        weight = held * jnp.broadcast_to(infos[pl.ds(e, 1), :], (8, RW))[:, 2:3]
        mask = cover[pl.ds(e, 1), :]
        acc = [acc[k] + (right if k % 2 else left) * mask[:, k * RW : (k + 1) * RW] for k in range(out_blocks)]
        cnt = [cnt[k] + weight * mask[:, k * RW : (k + 1) * RW] for k in range(out_blocks)]
        return acc, cnt

    zero = [jnp.zeros((8, RW), F32)] * out_blocks
    acc, cnt = lax.fori_loop(0, 64, add_block, (zero, zero))
    for k in range(out_blocks):
        out[0, :, k * RW : (k + 1) * RW] = acc[k] / jnp.maximum(cnt[k], 1.0)


def on_device(
    coadd_image, science, row_offset, col_offset, intersections, visit_weight, basis_index, weights, profiles
):
    any_space = pl.BlockSpec(memory_space=pl.ANY)
    smem = pl.BlockSpec(memory_space=pltpu.SMEM)
    vmem = pl.BlockSpec(memory_space=pltpu.VMEM)
    dma = pltpu.SemaphoreType.DMA
    return pl.pallas_call(
        kernel,
        out_shape=jax.ShapeDtypeStruct((1, 8, 1024), F32),
        in_specs=[any_space, any_space, smem, smem, smem, smem, smem, smem, vmem],
        out_specs=vmem,
        scratch_shapes=[
            pltpu.VMEM((4, 4, 4, 8, 1024), F32),
            pltpu.VMEM((256, 256), F32),
            pltpu.VMEM((16, COLS), F32),
            pltpu.VMEM((COLS, 2 * B * RW), BF16),
            pltpu.VMEM((COLS, 2 * B * RW), BF16),
            pltpu.VMEM((2 * B, 2 * RW, ROWS), BF16),
            pltpu.VMEM((2 * B, 2 * RW, ROWS), BF16),
            pltpu.VMEM((32, 8, 256), F32),
            pltpu.VMEM((64, 8, 256), F32),
            pltpu.VMEM((4, 4, 4, 1, 128), F32),
            pltpu.VMEM((64, 128), F32),
            pltpu.VMEM((64, 1024), F32),
            pltpu.VMEM((64, 128), F32),
            pltpu.VMEM((64, 1, 128), F32),
            pltpu.VMEM((4, 2, 128), F32),
            dma((2,)),
            dma((NPART, 3, 3)),
            dma((NPART, 3, 3)),
            dma((3, 3)),
            dma((3, 3)),
            dma((3,)),
            dma((3,)),
            dma((2,)),
            dma((2,)),
        ],
        compiler_params=pltpu.CompilerParams(
            collective_id=0, has_side_effects=True, vmem_limit_bytes=40 * 1024 * 1024
        ),
        name="difference",
    )(coadd_image, science, row_offset, col_offset, intersections, visit_weight, basis_index, weights, profiles)


def solution(mesh):
    return jax.shard_map(
        on_device,
        mesh=mesh,
        in_specs=(
            P("tile", "epoch", None),
            P("tile", "epoch", None, None),
            P("tile", "epoch"),
            P("tile", "epoch"),
            P("tile", "epoch"),
            P("tile", "epoch"),
            P("tile", "epoch", None, None, None),
            P("tile", "epoch", None, None, None),
            P(),
        ),
        out_specs=P("tile", "epoch", None),
        check_vma=False,
    )
```

time: 1120 us -> 61.6 us (0.06)
  the two profiles are of different devices: /device:TPU:0 before, /device:TPU:1 now
where the time goes in v1:
time: 61.6 us; the launch traced here: 61.4 us
  Pallas kernels  55.6 us (90%)
  local copies, waits for them, and re-layouts  3.11 us (5%)
  between operations  2.62 us (4%)
    pallas_call x1, Pallas kernels, on_device(): pl.pallas_call(kernel, out_shape=jax.ShapeDtypeStruct((1, 8, 1024), F32),...  55.6 us
    unnamed x10, local copies, waits for them, and re-layouts  3.11 us

profile of v1, /device:TPU:1, one launch (start us, length us, event | category | flops | bytes accessed | tf_op | source)
XLA Modules:
  0.0 61.4 jit_solution(14668190081505218652)
XLA Ops:
  0.0 0.0 copy-start.2
  2.6 0.0 copy-start.3
  2.6 0.8 %copy.10.basis_index = s32[1,1,2,3,2]{4,3,2,1,0:T(4,128)S(1)} copy(s32[1,1,2,3,2]{3,4,2,1,0:T(2,128)} %param.15) | data formatting | bytes 96 | tf_op args[6]
  3.4 0.0 copy-done.2
  3.4 0.0 copy-done.3
  3.4 0.0 copy-start
  3.4 0.9 %copy-done = f32[1,1,256,256]{3,2,1,0:T(8,128)S(1)} copy-done((f32[1,1,256,256]{3,2,1,0:T(8,128)S(1)}, f32[1,1,256,256]{3,2,1,0:T(8,128)}, u32[]{:S(2)}) %copy-start) | copy-done | bytes 262168
  4.4 0.0 copy-start.1
  4.4 0.8 %copy-done.1 = f32[1,8,1024]{2,1,0:T(8,128)S(1)} copy-done((f32[1,8,1024]{2,1,0:T(8,128)S(1)}, f32[1,8,1024]{2,1,0:T(8,128)}, u32[]{:S(2)}) %copy-start.1) | copy-done | bytes 32792
  5.1 55.6 %difference.1 = f32[1,8,1024]{2,1,0:T(8,128)S(1)} custom-call(f32[1,8,1024]{2,1,0:T(8,128)S(1)} %copy-done.1, f32[1,1,256,256]{3,2,1,0:T(8,128)S(1)} %copy-done, s32[1,1]{1,0:T(1,128)S(6)} %copy.12.row_offset, s32[1,1]{1,0:T(1,128)S(6)} %copy.13.col_offset, s32[1,1]{1,0:T(1,128)S(6)} %copy.14.intersections, f32[1,1]{1,0:T(1,128)S(6)} %copy.15.visit_weight, ...), custom_call_target="tpu_custom_call" | custom-call | tf_op jit(solution)/shard_map/difference/pallas_call | solution.py:307
  60.7 0.6 %copy.16 = f32[1,8,1024]{2,1,0:T(8,128)} copy(f32[1,8,1024]{2,1,0:T(8,128)S(1)} %difference.1) | data formatting | bytes 65536
Async XLA Ops:
  0.0 3.4 %copy-start.2 = (f32[16,31]{1,0:T(8,128)S(1)}, f32[16,31]{1,0:T(8,128)}, u32[]{:S(2)}) copy-start(f32[16,31]{1,0:T(8,128)} %profiles.1) | copy-start | bytes 5956
  2.6 0.8 %copy-start.3 = (f32[1,1,2,2,3]{4,3,2,1,0:T(2,128)S(1)}, f32[1,1,2,2,3]{4,3,2,1,0:T(2,128)}, u32[]{:S(2)}) copy-start(f32[1,1,2,2,3]{4,3,2,1,0:T(2,128)} %weights.1) | copy-start | bytes 148
  3.4 1.0 %copy-start = (f32[1,1,256,256]{3,2,1,0:T(8,128)S(1)}, f32[1,1,256,256]{3,2,1,0:T(8,128)}, u32[]{:S(2)}) copy-start(f32[1,1,256,256]{3,2,1,0:T(8,128)} %science.1) | copy-start | bytes 786436
  4.4 0.8 %copy-start.1 = (f32[1,8,1024]{2,1,0:T(8,128)S(1)}, f32[1,8,1024]{2,1,0:T(8,128)}, u32[]{:S(2)}) copy-start(f32[1,8,1024]{2,1,0:T(8,128)} %coadd.1) | copy-start | bytes 98308

commit v2 on v1

v2 whole, which is shorter than its diff:
```python
import jax
import jax.numpy as jnp
from jax import lax
from jax.experimental import pallas as pl
from jax.experimental.pallas import tpu as pltpu
from jax.sharding import PartitionSpec as P

KW = 31
HALF = 15
RW = 128
B = 3
F32 = jnp.float32
BF16 = jnp.bfloat16
MESH = pl.DeviceIdType.MESH

STRIDES = (16, 4, 1)
PARTS = (
    (0, 384, (1, 2, 0)),
    (384, 384, (1, 0, 2)),
    (768, 256, (2, 0, 1)),
)
NPART = len(PARTS)
ROWS = 384
COLS = 512


def split(value):
    high = value.astype(BF16)
    return high, (value - high.astype(F32)).astype(BF16)


def roll_by(value, amount, axis, limit=None):
    chosen = jnp.broadcast_to(amount, value.shape)
    step = 1
    while step < value.shape[axis]:
        value = jnp.where((chosen & step) != 0, pltpu.roll(value, step, axis), value)
        step *= 2
    return value


def toeplitz(taps, shift, rows):
    width = taps.shape[1]
    base = roll_by(jnp.broadcast_to(taps, (8, width)), shift & 511, 1)
    return pltpu.roll(jnp.broadcast_to(base[0:1, :], (rows, width)), 0, 1, stride=1, stride_axis=0)


def folded_toeplitz(taps, shift, rows, turn):
    row = lax.broadcasted_iota(jnp.int32, (rows, taps.shape[1]), 0)
    return jnp.where(row < turn, toeplitz(taps, shift - turn + rows, rows), toeplitz(taps, shift - turn, rows))


def pick(pieces, start, keep):
    chosen = jnp.broadcast_to(start, pieces[0].shape)
    step = 1
    while step * 2 <= len(pieces) - keep:
        step *= 2
    while step:
        moved = (chosen & step) != 0
        count = min(len(pieces), keep + step - 1)
        pieces = [
            jnp.where(moved, pieces[j + step], pieces[j]) if j + step < len(pieces) else pieces[j]
            for j in range(count)
        ]
        step //= 2
    return pieces


def kernel(
    coadd, science, row_offset, col_offset, intersections, visit_weight, basis_index, weights, profiles,
    out,
    tile, sci, prof, table, hor, ver, sumband, slots, recv, info, infos, cover, held, sums,
    row_s, col_s, int_s, vis_s, bas_s, wei_s,
    local_sem, send_sem, recv_sem, info_send, info_recv, sum_send, sum_recv, a2a_send, a2a_recv,
):
    me_t = lax.axis_index("tile")
    me = lax.axis_index("epoch")
    coord = (me // 16, (me // 4) % 4, me % 4)

    own_copy = pltpu.make_async_copy(coadd.at[0], tile.at[coord[0], coord[1], coord[2]], local_sem.at[0])
    own_copy.start()
    pairs = (
        (row_offset, row_s), (col_offset, col_s), (intersections, int_s), (visit_weight, vis_s),
        (basis_index, bas_s), (weights, wei_s), (profiles, prof),
    )
    small = [pltpu.make_async_copy(src, dst, local_sem.at[2 + i]) for i, (src, dst) in enumerate(pairs)]
    for copy in small:
        copy.start()
    sci_copy = pltpu.make_async_copy(science.at[0, 0], sci, local_sem.at[1])
    sci_copy.start()

    def peer(axis, k):
        here = coord[axis]
        return me + (lax.rem(here + k, 4) - here) * STRIDES[axis]

    barrier = pltpu.get_barrier_semaphore()
    for axis in range(3):
        for k in (1, 2, 3):
            pl.semaphore_signal(barrier, inc=1, device_id={"epoch": peer(axis, k)}, device_id_type=MESH)
    for k in (1, 2, 3):
        pl.semaphore_signal(barrier, inc=1, device_id={"tile": lax.rem(me_t + k, 4)}, device_id_type=MESH)

    table[...] = jnp.zeros_like(table)
    for copy in small:
        copy.wait()
    oy = row_s[0, 0]
    ox = col_s[0, 0]
    flag = int_s[0, 0].astype(F32)
    gain = flag * vis_s[0, 0]
    lane = lax.broadcasted_iota(jnp.int32, (1, 128), 1)
    info[coord[0], coord[1], coord[2]] = jnp.where(
        lane == 0, oy.astype(F32), jnp.where(lane == 1, ox.astype(F32), gain)
    )
    table[:, 0:KW] = prof[...]
    own_copy.wait()
    pl.semaphore_wait(barrier, 12)

    def stage_copies(buffer, cols, order, stage, sends, recvs):
        axis = order[stage]
        where = tuple(slice(None) if a in order[:stage] else coord[a] for a in range(3))
        block = buffer.at[where + ((slice(None),) if cols is None else (slice(None), pl.ds(*cols)))]
        return [
            pltpu.make_async_remote_copy(
                src_ref=block,
                dst_ref=block,
                send_sem=sends.at[k - 1],
                recv_sem=recvs.at[k - 1],
                device_id={"epoch": peer(axis, k)},
                device_id_type=MESH,
            )
            for k in (1, 2, 3)
        ]

    def part_copies(part, stage):
        lo, width, order = PARTS[part]
        return stage_copies(tile, (lo, width), order, stage, send_sem.at[part, stage], recv_sem.at[part, stage])

    def info_copies(stage):
        return stage_copies(info, None, (1, 2, 0), stage, info_send.at[stage], info_recv.at[stage])

    started = []

    def start_stage(stage):
        for part in range(NPART):
            if stage:
                for copy in part_copies(part, stage - 1):
                    copy.wait_recv()
            for copy in part_copies(part, stage):
                copy.start()
                started.append(copy)
        if stage:
            for copy in info_copies(stage - 1):
                copy.wait_recv()
        for copy in info_copies(stage):
            copy.start()
            started.append(copy)

    start_stage(0)

    row_block = jnp.minimum((oy - HALF) >> 6, (512 - ROWS) // 64)
    col_block = jnp.minimum((ox - HALF) >> 7, (1024 - COLS) // 128)
    row_shift = oy - HALF - 64 * row_block
    col_shift = ox - HALF - 128 * col_block
    row_turn = oy & 255
    col_turn = ox & 127

    profile = lax.broadcasted_iota(jnp.int32, (16, COLS), 0)

    def taps_of(index):
        return jnp.sum(jnp.where(profile == index, table[...], 0.0), axis=0, keepdims=True)

    across_sums, down_sums = [], []

    def make_horizontal(s):
        for b in range(B):
            band = folded_toeplitz(taps_of(bas_s[0, 0, s, 0, b]), col_shift + s * RW, RW, col_turn)
            across_sums.append(jnp.sum(band, axis=0, keepdims=True))
            high, low = split(band.T)
            at = pl.ds(b * RW, RW)
            hor[s, 0:COLS, at] = high
            hor[s, COLS : 2 * COLS, at] = low
            hor[s, 2 * COLS : 3 * COLS, at] = high

    def make_vertical(s):
        row = lax.broadcasted_iota(jnp.int32, (2 * RW, 1), 0)
        upper = ((row - row_turn) & 255) < RW
        for b in range(B):
            taps = taps_of(bas_s[0, 0, s, 1, b])
            band = folded_toeplitz(taps, row_shift, 2 * RW, row_turn)
            band = band * jnp.where(upper, wei_s[0, 0, 0, s, b], wei_s[0, 0, 1, s, b])
            band = band[:, 0:ROWS]
            down_sums.append(jnp.sum(band, axis=0, keepdims=True))
            high, low = split(band)
            at = 3 * b * ROWS
            ver[s, :, at : at + ROWS] = high
            ver[s, :, at + ROWS : at + 2 * ROWS] = high
            ver[s, :, at + 2 * ROWS : at + 3 * ROWS] = low

    make_horizontal(0)
    start_stage(1)
    make_horizontal(1)
    make_vertical(0)
    start_stage(2)
    make_vertical(1)

    pad = [jnp.zeros((1, ROWS), F32)] * 2, [jnp.zeros((1, COLS), F32)] * 2
    sumband[...] = lax.dot_general(
        jnp.concatenate(down_sums + pad[0], axis=0),
        jnp.concatenate(across_sums + pad[1], axis=0),
        (((0,), (0,)), ((), ())),
        precision=lax.Precision.HIGHEST,
        preferred_element_type=F32,
    )
    sci_copy.wait()
    science_sum = jnp.sum(sci[...], axis=0, keepdims=True)
    science_sum = science_sum[:, 0:RW] + science_sum[:, RW : 2 * RW]
    for s in range(2):
        at = slice(s * RW, (s + 1) * RW)
        sci[:, at] = roll_by(roll_by(sci[:, at], col_turn, 1), row_turn, 0)

    for part in range(NPART):
        for copy in part_copies(part, 2):
            copy.wait_recv()

    window = pick([tile[:, :, :, :, j * 128 : (j + 1) * 128].reshape(8, 64, 128) for j in range(8)], col_block, 4)
    window = jnp.concatenate([piece.reshape(512, 128) for piece in window], axis=1)
    window = pick([window[j * 64 : (j + 1) * 64] for j in range(8)], row_block, 6)
    window = jnp.concatenate(window, axis=0)
    model_sum = jnp.sum(window * sumband[...], axis=0, keepdims=True)
    total = science_sum
    for j in range(4):
        total = total - model_sum[:, j * 128 : (j + 1) * 128]
    sums[me_t] = jnp.where(
        lax.broadcasted_iota(jnp.int32, (2, RW), 0) == 0, jnp.sum(total) * flag, flag
    )
    sum_copies = [
        pltpu.make_async_remote_copy(
            src_ref=sums.at[me_t],
            dst_ref=sums.at[me_t],
            send_sem=sum_send.at[k - 1],
            recv_sem=sum_recv.at[k - 1],
            device_id={"tile": lax.rem(me_t + k, 4)},
            device_id_type=MESH,
        )
        for k in (1, 2, 3)
    ]
    for copy in sum_copies:
        copy.start()

    win_hi, win_lo = split(window)
    win_all = jnp.concatenate([win_hi, win_hi, win_lo], axis=1)
    level = None
    for s in range(2):
        across = jnp.dot(win_all, hor[s], preferred_element_type=F32)
        stack = []
        for b in range(B):
            x_hi, x_lo = split(across[:, b * RW : (b + 1) * RW])
            stack += [x_hi, x_lo, x_hi]
        model = jnp.dot(ver[s], jnp.concatenate(stack, axis=0), preferred_element_type=F32)
        if s == 0:
            for copy in sum_copies:
                copy.wait_recv()
            both = (sums[0] + sums[1]) + (sums[2] + sums[3])
            level = both[0:1, :] / jnp.maximum(both[1:2, :] * 65536.0, 1.0)
        difference = (sci[:, s * RW : (s + 1) * RW] - model - level) * gain
        slots[s] = difference.reshape(32, 8, RW)

        def send_block(k, carry, s=s):
            target = lax.rem(me + k, 64)
            pltpu.make_async_remote_copy(
                src_ref=slots.at[s, lax.rem(target, 32)],
                dst_ref=recv.at[s, me],
                send_sem=a2a_send.at[s],
                recv_sem=a2a_recv.at[s],
                device_id={"epoch": target},
                device_id_type=MESH,
            ).start()
            return carry

        lax.fori_loop(1, 64, send_block, 0)
        recv[s, me] = slots[s, lax.rem(me, 32)]

    for copy in info_copies(2):
        copy.wait_recv()
    for e in range(64):
        infos[e : e + 1, :] = info[e // 16, (e // 4) % 4, e % 4]
    every = infos[...]
    column = lax.broadcasted_iota(jnp.int32, (64, 1024), 1).astype(F32)
    first = every[:, 1:2]
    for s in range(2):
        least = first + float(s * RW)
        cover[s] = jnp.where((column >= least) & (column < least + float(RW)), 1.0, 0.0)
    row = (me * 8 + lax.broadcasted_iota(jnp.int32, (64, 8), 1)).astype(F32)
    first = every[:, 0:1]
    inside = (row >= first) & (row < first + 256.0)
    count = lax.dot_general(
        jnp.where(inside, every[:, 2:3], 0.0),
        cover[0] + cover[1],
        (((0,), (0,)), ((), ())),
        precision=lax.Precision.HIGHEST,
        preferred_element_type=F32,
    )
    scale = 1.0 / jnp.maximum(count, 1.0)
    my_row = (me * 8 + lax.broadcasted_iota(jnp.int32, (8, RW), 0)).astype(F32)

    def make_held(e, carry):
        first_row = jnp.broadcast_to(infos[pl.ds(e, 1), 0:1], (8, RW))
        held[e] = jnp.where((my_row >= first_row) & (my_row < first_row + 256.0), 1.0, 0.0)
        return carry

    lax.fori_loop(0, 64, make_held, 0, unroll=8)

    for copy in started:
        copy.wait_send()
    for copy in sum_copies:
        copy.wait_send()

    def wait_for(ref, sem):
        pltpu.make_async_copy(ref, ref, sem).wait()

    acc = [jnp.zeros((8, RW), F32)] * 8
    for s in range(2):
        wait_for(recv.at[s, pl.ds(0, 63)], a2a_recv.at[s])

        def add_block(e, acc, s=s):
            block = recv[s, e] * held[e]
            mask = cover[s, pl.ds(e, 1), :]
            return [acc[k] + block * mask[:, k * RW : (k + 1) * RW] for k in range(8)]

        acc = lax.fori_loop(0, 64, add_block, acc, unroll=8)
    for k in range(8):
        out[0, :, k * RW : (k + 1) * RW] = acc[k] * scale[:, k * RW : (k + 1) * RW]
    for s in range(2):
        wait_for(recv.at[s, pl.ds(0, 63)], a2a_send.at[s])


def on_device(
    coadd_image, science, row_offset, col_offset, intersections, visit_weight, basis_index, weights, profiles
):
    any_space = pl.BlockSpec(memory_space=pl.ANY)
    dma = pltpu.SemaphoreType.DMA
    return pl.pallas_call(
        kernel,
        out_shape=jax.ShapeDtypeStruct((1, 8, 1024), F32),
        in_specs=[any_space] * 9,
        out_specs=pl.BlockSpec(memory_space=pltpu.VMEM),
        scratch_shapes=[
            pltpu.VMEM((4, 4, 4, 8, 1024), F32),
            pltpu.VMEM((256, 256), F32),
            pltpu.VMEM((16, KW), F32),
            pltpu.VMEM((16, COLS), F32),
            pltpu.VMEM((2, 3 * COLS, B * RW), BF16),
            pltpu.VMEM((2, 2 * RW, 3 * B * ROWS), BF16),
            pltpu.VMEM((ROWS, COLS), F32),
            pltpu.VMEM((2, 32, 8, RW), F32),
            pltpu.VMEM((2, 64, 8, RW), F32),
            pltpu.VMEM((4, 4, 4, 1, 128), F32),
            pltpu.VMEM((64, 128), F32),
            pltpu.VMEM((2, 64, 1024), F32),
            pltpu.VMEM((64, 8, RW), F32),
            pltpu.VMEM((4, 2, 128), F32),
            pltpu.SMEM((1, 1), jnp.int32),
            pltpu.SMEM((1, 1), jnp.int32),
            pltpu.SMEM((1, 1), jnp.int32),
            pltpu.SMEM((1, 1), F32),
            pltpu.SMEM((1, 1, 2, 2, B), jnp.int32),
            pltpu.SMEM((1, 1, 2, 2, B), F32),
            dma((9,)),
            dma((NPART, 3, 3)),
            dma((NPART, 3, 3)),
            dma((3, 3)),
            dma((3, 3)),
            dma((3,)),
            dma((3,)),
            dma((2,)),
            dma((2,)),
        ],
        compiler_params=pltpu.CompilerParams(
            collective_id=0, has_side_effects=True, vmem_limit_bytes=60 * 1024 * 1024
        ),
        name="difference",
    )(
        coadd_image, science, row_offset, col_offset, intersections, visit_weight,
        jnp.swapaxes(basis_index, 3, 4), weights, profiles,
    )


def solution(mesh):
    return jax.shard_map(
        on_device,
        mesh=mesh,
        in_specs=(
            P("tile", "epoch", None),
            P("tile", "epoch", None, None),
            P("tile", "epoch"),
            P("tile", "epoch"),
            P("tile", "epoch"),
            P("tile", "epoch"),
            P("tile", "epoch", None, None, None),
            P("tile", "epoch", None, None, None),
            P(),
        ),
        out_specs=P("tile", "epoch", None),
        check_vma=False,
    )
```

time: 61.6 us -> 53.6 us (0.87)
  Pallas kernels: 55.6 us -> 49.4 us
  local copies, waits for them, and re-layouts: 3.11 us -> 1.38 us
    pallas_call x1, Pallas kernels: 55.6 us -> 49.4 us  [on_device(): pl.pallas_call(kernel, out_shape=jax.ShapeDtypeStruct((1, 8, 1024), F32),...]
    unnamed x10 -> x1, local copies, waits for them, and re-layouts: 3.11 us -> 1.38 us
where the time goes in v2:
time: 53.6 us; the launch traced here: 53.4 us
  Pallas kernels  49.4 us (92%)
  between operations  2.59 us (5%)
  local copies, waits for them, and re-layouts  1.38 us (3%)
    pallas_call x1, Pallas kernels, on_device(): pl.pallas_call(kernel, out_shape=jax.ShapeDtypeStruct((1, 8, 1024), F32),...  49.4 us
    unnamed x1, local copies, waits for them, and re-layouts  1.38 us

profile of v2, /device:TPU:1, one launch (start us, length us, event | category | flops | bytes accessed | tf_op | source)
XLA Modules:
  0.0 53.4 jit_solution(17682016553147859574)
XLA Ops:
  2.6 49.4 %difference.1 = f32[1,8,1024]{2,1,0:T(8,128)} custom-call(f32[1,8,1024]{2,1,0:T(8,128)} %coadd.1, f32[1,1,256,256]{3,2,1,0:T(8,128)} %science.1, s32[1,1]{1,0:T(1,128)S(6)} %copy.11.row_offset, s32[1,1]{1,0:T(1,128)S(6)} %copy.12.col_offset, s32[1,1]{1,0:T(1,128)S(6)} %copy.13.intersections, f32[1,1]{1,0:T(1,128)S(6)} %copy.14.visit_weight, ...), custom_call_target="tpu_custom_call" | custom-call | tf_op jit(solution)/shard_map/difference/pallas_call | solution.py:341
  52.0 1.4 %copy.15 = f32[1,8,1024]{2,1,0:T(8,128)} copy(f32[1,8,1024]{2,1,0:T(8,128)} %difference.1) | data formatting | bytes 65536

commit v3 on v0

v3 whole, which is shorter than its diff:
```python
import jax
import jax.numpy as jnp
from jax import lax
from jax.experimental import pallas as pl
from jax.experimental.pallas import tpu as pltpu
from jax.sharding import PartitionSpec as P

KW = 31
HALF = 15
RW = 128
B = 3
NPROF = 16
PAIRS = NPROF * NPROF
F32 = jnp.float32
BF16 = jnp.bfloat16
MESH = pl.DeviceIdType.MESH


def split(value):
    high = value.astype(BF16)
    return high, (value - high.astype(F32)).astype(BF16)


def roll_by(value, amount, axis):
    chosen = jnp.broadcast_to(amount, value.shape)
    step = 1
    while step < value.shape[axis]:
        value = jnp.where((chosen & step) != 0, pltpu.roll(value, step, axis), value)
        step *= 2
    return value


def wide_dot(a, b):
    high, low = split(a)
    return jnp.dot(
        jnp.concatenate([high, low], axis=1), jnp.concatenate([b, b], axis=0), preferred_element_type=F32
    )


def kernel(
    coadd, science, row_offset, col_offset, intersections, visit_weight, basis_index, weights, profiles,
    out,
    near, sci, prof, table, hor, pairs, pairs_hi, pairs_lo, slots, recv, given, params, masks, model,
    parts, sums,
    row_s, col_s, int_s, vis_s, bas_s, wei_s,
    local_sem, halo_send, halo_recv, sum_send, sum_recv, par_sem, sci_sem, lev_sem,
):
    me_t = lax.axis_index("tile")
    me = lax.axis_index("epoch")

    arrays = (
        (row_offset, row_s), (col_offset, col_s), (intersections, int_s), (visit_weight, vis_s),
        (basis_index, bas_s), (weights, wei_s), (profiles, prof),
    )
    small = [pltpu.make_async_copy(src, dst, local_sem.at[2 + i]) for i, (src, dst) in enumerate(arrays)]
    for copy in small:
        copy.start()
    sci_copy = pltpu.make_async_copy(science.at[0, 0], sci, local_sem.at[1])
    sci_copy.start()
    own_copy = pltpu.make_async_copy(coadd.at[0], near.at[2], local_sem.at[0])
    own_copy.start()

    barrier = pltpu.get_barrier_semaphore()

    def greet(k, carry):
        pl.semaphore_signal(barrier, inc=1, device_id={"epoch": lax.rem(me + k, 64)}, device_id_type=MESH)
        return carry

    lax.fori_loop(1, 64, greet, 0)
    for k in (1, 2, 3):
        pl.semaphore_signal(barrier, inc=1, device_id={"tile": lax.rem(me_t + k, 4)}, device_id_type=MESH)

    for copy in small:
        copy.wait()
    oy = row_s[0, 0]
    ox = col_s[0, 0]
    flag = int_s[0, 0].astype(F32)
    gain = flag * vis_s[0, 0]

    lane = lax.broadcasted_iota(jnp.int32, (2, 128), 1)
    region = lax.broadcasted_iota(jnp.int32, (2, 128), 0)

    def by_region(left, right):
        return jnp.where(region == 0, left, right)

    entries = [oy.astype(F32), by_region(ox.astype(F32), ox.astype(F32) + float(RW)), gain, flag]
    for b in range(B):
        pair = [(bas_s[0, 0, s, 0, b] * NPROF + bas_s[0, 0, s, 1, b]).astype(F32) for s in range(2)]
        entries.append(by_region(*pair))
    for y in range(2):
        for b in range(B):
            entries.append(by_region(wei_s[0, 0, y, 0, b], wei_s[0, 0, y, 1, b]))
    row = jnp.zeros((2, 128), F32)
    for k, entry in enumerate(entries):
        row = jnp.where(lane == k, entry, row)
    given[me] = row

    sci_copy.wait()
    image = sci[...]
    science_sum = jnp.sum(image)
    slots[...] = (roll_by(roll_by(image, ox & 255, 1), oy & 255, 0) * gain).reshape(32, 8, 256)
    own_copy.wait()
    pl.semaphore_wait(barrier, 66)

    def send_params(k, carry):
        pltpu.make_async_remote_copy(
            src_ref=given.at[me],
            dst_ref=given.at[me],
            send_sem=par_sem.at[0],
            recv_sem=par_sem.at[1],
            device_id={"epoch": lax.rem(me + k, 64)},
            device_id_type=MESH,
        ).start()
        return carry

    def send_science(k, carry):
        target = lax.rem(me + k, 64)
        pltpu.make_async_remote_copy(
            src_ref=slots.at[lax.rem(target, 32)],
            dst_ref=recv.at[me],
            send_sem=sci_sem.at[0],
            recv_sem=sci_sem.at[1],
            device_id={"epoch": target},
            device_id_type=MESH,
        ).start()
        return carry

    halo = [
        pltpu.make_async_remote_copy(
            src_ref=near.at[2],
            dst_ref=near.at[2 - d],
            send_sem=halo_send.at[i],
            recv_sem=halo_recv.at[i],
            device_id={"epoch": lax.rem(me + d + 64, 64)},
            device_id_type=MESH,
        )
        for i, d in enumerate((1, -1, 2, -2))
    ]
    for copy in halo:
        copy.start()
    lax.fori_loop(1, 64, send_params, 0)
    lax.fori_loop(1, 64, send_science, 0)
    recv[me] = slots[lax.rem(me, 32)]

    table[...] = jnp.zeros_like(table)
    table[:, 0:KW] = prof[...]
    wide = table[:, 0:128]
    vertical = jnp.concatenate([pltpu.roll(wide, r + 1, 1) for r in range(8)], axis=0)[:, 0:40]
    for q in range(NPROF):
        band = pltpu.roll(
            jnp.broadcast_to(table[q : q + 1, :], (RW, 2 * RW)), 0, 1, stride=1, stride_axis=0
        ).T
        high, low = split(band)
        at = slice(q * RW, (q + 1) * RW)
        hor[0 : 2 * RW, at] = high
        hor[2 * RW : 4 * RW, at] = low
        hor[4 * RW : 6 * RW, at] = high

    for copy in halo:
        copy.wait_recv()
    down = jnp.dot(
        vertical, near[...].reshape(40, 1024), precision=lax.Precision.HIGHEST, preferred_element_type=F32
    )
    down = pltpu.roll(down, HALF, 1)
    high, low = split(down)

    def stacked(value):
        def block(j):
            return value[:, (j % 8) * RW : (j % 8 + 1) * RW]

        return jnp.concatenate(
            [jnp.concatenate([block(j), block(j + 1)], axis=1) for j in range(8)], axis=0
        )

    high, low = stacked(high), stacked(low)
    left = jnp.concatenate([high, high, low], axis=1)
    for step in range(NPROF // 2):
        both = jnp.dot(left, hor[:, step * 256 : (step + 1) * 256], preferred_element_type=F32)
        for half in range(2):
            q = 2 * step + half
            at = slice(q * NPROF, (q + 1) * NPROF)
            for j in range(8):
                cols = slice(j * RW, (j + 1) * RW)
                for r in range(8):
                    top = j * 128 + r * NPROF
                    piece = both[top : top + NPROF, half * RW : (half + 1) * RW]
                    pairs[r, at, cols] = piece
                    high, low = split(piece)
                    pairs_hi[r, at, cols] = high
                    pairs_lo[r, at, cols] = low

    def wait_for(ref, sem):
        pltpu.make_async_copy(ref, ref, sem).wait()

    most = pl.ds(0, 63)
    wait_for(given.at[most], par_sem.at[1])
    for e in range(64):
        params[2 * e : 2 * e + 2, :] = given[e]
    every = params[...]
    across = every.T

    def entry(k):
        return across[k : k + 1, :]

    first = every[:, 1:2]
    column = lax.broadcasted_iota(jnp.int32, (128, 1024), 1).astype(F32)
    cover = jnp.where((column >= first) & (column < first + float(RW)), 1.0, 0.0).astype(BF16)
    column = lax.broadcasted_iota(jnp.int32, (1024, 128), 0).astype(F32)
    cover_t = jnp.where((column >= entry(1)) & (column < entry(1) + float(RW)), 1.0, 0.0).astype(BF16)
    my_row = (me * 8 + lax.broadcasted_iota(jnp.int32, (8, 128), 0)).astype(F32)
    inside = my_row - entry(0)
    upper = jnp.where((inside >= 0.0) & (inside < 128.0), 1.0, 0.0)
    lower = jnp.where((inside >= 128.0) & (inside < 256.0), 1.0, 0.0)

    pair_id = lax.broadcasted_iota(jnp.int32, (PAIRS, 128), 0).astype(F32)
    weight = [jnp.zeros((PAIRS, 128), F32)] * 2
    for b in range(B):
        same = pair_id == entry(4 + b)
        weight = [weight[y] + jnp.where(same, entry(7 + 3 * y + b), 0.0) for y in range(2)]

    def weight_of(r):
        return weight[0] * upper[r : r + 1, :] + weight[1] * lower[r : r + 1, :]

    cover_t2 = jnp.concatenate([cover_t, cover_t], axis=0)
    model_sum = jnp.zeros((1, 128), F32)
    for r in range(8):
        z = jnp.concatenate([pairs_hi[r], pairs_lo[r]], axis=1)
        covered = jnp.dot(z, cover_t2, preferred_element_type=F32)
        model_sum = model_sum + jnp.sum(covered * weight_of(r), axis=0, keepdims=True)
    lane = lax.broadcasted_iota(jnp.int32, (1, 128), 1)
    parts[me] = jnp.where(lane == 2 * me, science_sum, 0.0) - model_sum

    def send_parts(k, carry):
        pltpu.make_async_remote_copy(
            src_ref=parts.at[me],
            dst_ref=parts.at[me],
            send_sem=lev_sem.at[0],
            recv_sem=lev_sem.at[1],
            device_id={"epoch": lax.rem(me + k, 64)},
            device_id_type=MESH,
        ).start()
        return carry

    lax.fori_loop(1, 64, send_parts, 0)

    for r in range(8):
        coef = wide_dot(weight_of(r) * entry(2), cover)
        model[r : r + 1, :] = jnp.sum(pairs[r] * coef, axis=0, keepdims=True)
    count = wide_dot((upper + lower) * entry(2), cover)
    scale = 1.0 / jnp.maximum(count, 1.0)

    column = lax.broadcasted_iota(jnp.int32, (8, 1024), 1).astype(F32)
    rows = (me * 8 + lax.broadcasted_iota(jnp.int32, (8, 1024), 0)).astype(F32)

    def make_mask(e, carry):
        top = jnp.broadcast_to(given[e, 0:1, 0:1], (8, 1024))
        side = jnp.broadcast_to(given[e, 0:1, 1:2], (8, 1024))
        hit = (rows >= top) & (rows < top + 256.0) & (column >= side) & (column < side + 256.0)
        masks[e] = jnp.where(hit, 1.0, 0.0)
        return carry

    lax.fori_loop(0, 64, make_mask, 0, unroll=4)

    wait_for(parts.at[most], lev_sem.at[1])
    total = jnp.sum(parts[...], axis=0)
    even = (lane & 1) == 0
    total = total + jnp.where(even, pltpu.roll(total, 127, 1), pltpu.roll(total, 1, 1))
    sums[me_t] = jnp.concatenate([total * entry(3), entry(3)], axis=0)
    sum_copies = [
        pltpu.make_async_remote_copy(
            src_ref=sums.at[me_t],
            dst_ref=sums.at[me_t],
            send_sem=sum_send.at[k - 1],
            recv_sem=sum_recv.at[k - 1],
            device_id={"tile": lax.rem(me_t + k, 4)},
            device_id_type=MESH,
        )
        for k in (1, 2, 3)
    ]
    for copy in sum_copies:
        copy.start()

    wait_for(recv.at[most], sci_sem.at[1])

    def add_block(e, acc):
        halves = [recv[e, :, 0:RW], recv[e, :, RW : 2 * RW]]
        return [acc[k] + halves[k % 2] * masks[e, :, k * RW : (k + 1) * RW] for k in range(8)]

    acc = lax.fori_loop(0, 64, add_block, [jnp.zeros((8, RW), F32)] * 8, unroll=8)

    for copy in sum_copies:
        copy.wait_recv()
    both = (sums[0] + sums[1]) + (sums[2] + sums[3])
    level = both[0:1, :] / jnp.maximum(both[1:2, :] * 65536.0, 1.0)
    taken = model[...] + wide_dot((upper + lower) * (entry(2) * level), cover)
    for k in range(8):
        at = slice(k * RW, (k + 1) * RW)
        out[0, :, at] = (acc[k] - taken[:, at]) * scale[:, at]

    for copy in halo:
        copy.wait_send()
    for copy in sum_copies:
        copy.wait_send()
    wait_for(given.at[most], par_sem.at[0])
    wait_for(recv.at[most], sci_sem.at[0])
    wait_for(parts.at[most], lev_sem.at[0])


def on_device(
    coadd_image, science, row_offset, col_offset, intersections, visit_weight, basis_index, weights, profiles
):
    any_space = pl.BlockSpec(memory_space=pl.ANY)
    dma = pltpu.SemaphoreType.DMA
    return pl.pallas_call(
        kernel,
        out_shape=jax.ShapeDtypeStruct((1, 8, 1024), F32),
        in_specs=[any_space] * 9,
        out_specs=pl.BlockSpec(memory_space=pltpu.VMEM),
        scratch_shapes=[
            pltpu.VMEM((5, 8, 1024), F32),
            pltpu.VMEM((256, 256), F32),
            pltpu.VMEM((NPROF, KW), F32),
            pltpu.VMEM((NPROF, 2 * RW), F32),
            pltpu.VMEM((6 * RW, NPROF * RW), BF16),
            pltpu.VMEM((8, PAIRS, 1024), F32),
            pltpu.VMEM((8, PAIRS, 1024), BF16),
            pltpu.VMEM((8, PAIRS, 1024), BF16),
            pltpu.VMEM((32, 8, 256), F32),
            pltpu.VMEM((64, 8, 256), F32),
            pltpu.VMEM((64, 2, 128), F32),
            pltpu.VMEM((128, 128), F32),
            pltpu.VMEM((64, 8, 1024), F32),
            pltpu.VMEM((8, 1024), F32),
            pltpu.VMEM((64, 1, 128), F32),
            pltpu.VMEM((4, 2, 128), F32),
            pltpu.SMEM((1, 1), jnp.int32),
            pltpu.SMEM((1, 1), jnp.int32),
            pltpu.SMEM((1, 1), jnp.int32),
            pltpu.SMEM((1, 1), F32),
            pltpu.SMEM((1, 1, 2, 2, B), jnp.int32),
            pltpu.SMEM((1, 1, 2, 2, B), F32),
            dma((9,)),
            dma((4,)),
            dma((4,)),
            dma((3,)),
            dma((3,)),
            dma((2,)),
            dma((2,)),
            dma((2,)),
        ],
        compiler_params=pltpu.CompilerParams(
            collective_id=0, has_side_effects=True, vmem_limit_bytes=60 * 1024 * 1024
        ),
        name="difference",
    )(
        coadd_image, science, row_offset, col_offset, intersections, visit_weight,
        jnp.swapaxes(basis_index, 3, 4), weights, profiles,
    )


def solution(mesh):
    return jax.shard_map(
        on_device,
        mesh=mesh,
        in_specs=(
            P("tile", "epoch", None),
            P("tile", "epoch", None, None),
            P("tile", "epoch"),
            P("tile", "epoch"),
            P("tile", "epoch"),
            P("tile", "epoch"),
            P("tile", "epoch", None, None, None),
            P("tile", "epoch", None, None, None),
            P(),
        ),
        out_specs=P("tile", "epoch", None),
        check_vma=False,
    )
```

time: 1120 us -> 44.3 us (0.04)
  the two profiles are of different devices: /device:TPU:0 before, /device:TPU:1 now
where the time goes in v3:
time: 44.3 us; the launch traced here: 44.2 us
  Pallas kernels  40.2 us (91%)
  between operations  2.59 us (6%)
  local copies, waits for them, and re-layouts  1.38 us (3%)
    pallas_call x1, Pallas kernels, on_device(): pl.pallas_call(kernel, out_shape=jax.ShapeDtypeStruct((1, 8, 1024), F32),...  40.2 us
    unnamed x1, local copies, waits for them, and re-layouts  1.38 us

profile of v3, /device:TPU:1, one launch (start us, length us, event | category | flops | bytes accessed | tf_op | source)
XLA Modules:
  0.0 44.2 jit_solution(5423542743104686495)
XLA Ops:
  2.6 40.2 %difference.1 = f32[1,8,1024]{2,1,0:T(8,128)} custom-call(f32[1,8,1024]{2,1,0:T(8,128)} %coadd.1, f32[1,1,256,256]{3,2,1,0:T(8,128)} %science.1, s32[1,1]{1,0:T(1,128)S(6)} %copy.11.row_offset, s32[1,1]{1,0:T(1,128)S(6)} %copy.12.col_offset, s32[1,1]{1,0:T(1,128)S(6)} %copy.13.intersections, f32[1,1]{1,0:T(1,128)S(6)} %copy.14.visit_weight, ...), custom_call_target="tpu_custom_call" | custom-call | tf_op jit(solution)/shard_map/difference/pallas_call | solution.py:314
  42.8 1.4 %copy.15 = f32[1,8,1024]{2,1,0:T(8,128)} copy(f32[1,8,1024]{2,1,0:T(8,128)} %difference.1) | data formatting | bytes 65536

commit v4 on v3

--- a/solution.py
+++ b/solution.py
@@ -40,7 +40,7 @@
 def kernel(
     coadd, science, row_offset, col_offset, intersections, visit_weight, basis_index, weights, profiles,
     out,
-    near, sci, prof, table, hor, pairs, pairs_hi, pairs_lo, slots, recv, given, params, masks, model,
+    near, sci, prof, table, hor, pairs, slots, recv, given, params, masks, model,
     parts, sums,
     row_s, col_s, int_s, vis_s, bas_s, wei_s,
     local_sem, halo_send, halo_recv, sum_send, sum_recv, par_sem, sci_sem, lev_sem,
@@ -90,6 +90,9 @@
     for y in range(2):
         for b in range(B):
             entries.append(by_region(wei_s[0, 0, y, 0, b], wei_s[0, 0, y, 1, b]))
+    for pick in range(2):
+        for b in range(B):
+            entries.append(by_region(*[bas_s[0, 0, s, pick, b].astype(F32) for s in range(2)]))
     row = jnp.zeros((2, 128), F32)
     for k, entry in enumerate(entries):
         row = jnp.where(lane == k, entry, row)
@@ -146,11 +149,13 @@
     table[:, 0:KW] = prof[...]
     wide = table[:, 0:128]
     vertical = jnp.concatenate([pltpu.roll(wide, r + 1, 1) for r in range(8)], axis=0)[:, 0:40]
+    box = []
     for q in range(NPROF):
         band = pltpu.roll(
             jnp.broadcast_to(table[q : q + 1, :], (RW, 2 * RW)), 0, 1, stride=1, stride_axis=0
-        ).T
-        high, low = split(band)
+        )
+        box.append(jnp.sum(band, axis=0, keepdims=True))
+        high, low = split(band.T)
         at = slice(q * RW, (q + 1) * RW)
         hor[0 : 2 * RW, at] = high
         hor[2 * RW : 4 * RW, at] = low
@@ -161,6 +166,68 @@
     down = jnp.dot(
         vertical, near[...].reshape(40, 1024), precision=lax.Precision.HIGHEST, preferred_element_type=F32
     )
+    def wait_for(ref, sem):
+        pltpu.make_async_copy(ref, ref, sem).wait()
+
+    most = pl.ds(0, 63)
+    wait_for(given.at[most], par_sem.at[1])
+    for e in range(64):
+        params[2 * e : 2 * e + 2, :] = given[e]
+    every = params[...]
+    def field(k):
+        return every[:, k : k + 1]
+
+    profile = lax.broadcasted_iota(jnp.int32, (128, NPROF), 1).astype(F32)
+    chosen = jnp.concatenate([jnp.where(profile == field(13 + b), 1.0, 0.0) for b in range(B)], axis=0)
+    boxes = jnp.concatenate([jnp.concatenate(box, axis=0), jnp.zeros((NPROF, RW), F32)], axis=1)
+    taken = jnp.dot(chosen, boxes, precision=lax.Precision.HIGHEST, preferred_element_type=F32)
+    start = jnp.broadcast_to((field(1) - float(HALF)).astype(jnp.int32), (128, 128))
+    start = jnp.concatenate([start] * B, axis=0)
+    turn = jnp.concatenate([start] * 3, axis=1)
+    for step in (1, 2, 4, 8, 16, 32, 64):
+        taken = jnp.where((turn & step) != 0, pltpu.roll(taken, step, 1), taken)
+    block = start >> 7
+    spread = []
+    for j in range(8):
+        value = jnp.where(block == j, taken[:, 0:RW], 0.0)
+        for d in (1, 2):
+            if j >= d:
+                value = value + jnp.where(block == j - d, taken[:, d * RW : (d + 1) * RW], 0.0)
+        spread.append(value)
+    g_hi, g_lo = split(jnp.concatenate(spread, axis=1))
+    y_hi, y_lo = split(down)
+    caught = lax.dot_general(
+        jnp.concatenate([g_hi, g_hi, g_lo], axis=1),
+        jnp.concatenate([y_hi, y_lo, y_hi], axis=1),
+        (((1,), (1,)), ((), ())),
+        preferred_element_type=F32,
+    )
+    place = lax.broadcasted_iota(jnp.int32, (128, 128), 1)
+    offset = (me * 8 + (place >> 4)).astype(F32) - field(0)
+    place = (place & 15).astype(F32)
+    upper = (offset >= 0.0) & (offset < 128.0)
+    lower = (offset >= 128.0) & (offset < 256.0)
+    sum_of = jnp.zeros((128, 128), F32)
+    for b in range(B):
+        part = jnp.where(upper, field(7 + b), 0.0) + jnp.where(lower, field(10 + b), 0.0)
+        sum_of = sum_of + jnp.where(place == field(16 + b), part, 0.0) * caught[b * 128 : (b + 1) * 128]
+    model_sum = jnp.sum(sum_of.T, axis=0, keepdims=True)
+    lane = lax.broadcasted_iota(jnp.int32, (1, 128), 1)
+    parts[me] = jnp.where(lane == 2 * me, science_sum, 0.0) - model_sum
+
+    def send_parts(k, carry):
+        pltpu.make_async_remote_copy(
+            src_ref=parts.at[me],
+            dst_ref=parts.at[me],
+            send_sem=lev_sem.at[0],
+            recv_sem=lev_sem.at[1],
+            device_id={"epoch": lax.rem(me + k, 64)},
+            device_id_type=MESH,
+        ).start()
+        return carry
+
+    lax.fori_loop(1, 64, send_parts, 0)
+
     down = pltpu.roll(down, HALF, 1)
     high, low = split(down)
 
@@ -183,20 +250,8 @@
                 cols = slice(j * RW, (j + 1) * RW)
                 for r in range(8):
                     top = j * 128 + r * NPROF
-                    piece = both[top : top + NPROF, half * RW : (half + 1) * RW]
-                    pairs[r, at, cols] = piece
-                    high, low = split(piece)
-                    pairs_hi[r, at, cols] = high
-                    pairs_lo[r, at, cols] = low
-
-    def wait_for(ref, sem):
-        pltpu.make_async_copy(ref, ref, sem).wait()
-
-    most = pl.ds(0, 63)
-    wait_for(given.at[most], par_sem.at[1])
-    for e in range(64):
-        params[2 * e : 2 * e + 2, :] = given[e]
-    every = params[...]
+                    pairs[r, at, cols] = both[top : top + NPROF, half * RW : (half + 1) * RW]
+
     across = every.T
 
     def entry(k):
@@ -205,8 +260,6 @@
     first = every[:, 1:2]
     column = lax.broadcasted_iota(jnp.int32, (128, 1024), 1).astype(F32)
     cover = jnp.where((column >= first) & (column < first + float(RW)), 1.0, 0.0).astype(BF16)
-    column = lax.broadcasted_iota(jnp.int32, (1024, 128), 0).astype(F32)
-    cover_t = jnp.where((column >= entry(1)) & (column < entry(1) + float(RW)), 1.0, 0.0).astype(BF16)
     my_row = (me * 8 + lax.broadcasted_iota(jnp.int32, (8, 128), 0)).astype(F32)
     inside = my_row - entry(0)
     upper = jnp.where((inside >= 0.0) & (inside < 128.0), 1.0, 0.0)
@@ -220,34 +273,6 @@
 
     def weight_of(r):
         return weight[0] * upper[r : r + 1, :] + weight[1] * lower[r : r + 1, :]
-
-    cover_t2 = jnp.concatenate([cover_t, cover_t], axis=0)
-    model_sum = jnp.zeros((1, 128), F32)
-    for r in range(8):
-        z = jnp.concatenate([pairs_hi[r], pairs_lo[r]], axis=1)
-        covered = jnp.dot(z, cover_t2, preferred_element_type=F32)
-        model_sum = model_sum + jnp.sum(covered * weight_of(r), axis=0, keepdims=True)
-    lane = lax.broadcasted_iota(jnp.int32, (1, 128), 1)
-    parts[me] = jnp.where(lane == 2 * me, science_sum, 0.0) - model_sum
-
-    def send_parts(k, carry):
-        pltpu.make_async_remote_copy(
-            src_ref=parts.at[me],
-            dst_ref=parts.at[me],
-            send_sem=lev_sem.at[0],
-            recv_sem=lev_sem.at[1],
-            device_id={"epoch": lax.rem(me + k, 64)},
-            device_id_type=MESH,
-        ).start()
-        return carry
-
-    lax.fori_loop(1, 64, send_parts, 0)
-
-    for r in range(8):
-        coef = wide_dot(weight_of(r) * entry(2), cover)
-        model[r : r + 1, :] = jnp.sum(pairs[r] * coef, axis=0, keepdims=True)
-    count = wide_dot((upper + lower) * entry(2), cover)
-    scale = 1.0 / jnp.maximum(count, 1.0)
 
     column = lax.broadcasted_iota(jnp.int32, (8, 1024), 1).astype(F32)
     rows = (me * 8 + lax.broadcasted_iota(jnp.int32, (8, 1024), 0)).astype(F32)
@@ -280,6 +305,12 @@
     for copy in sum_copies:
         copy.start()
 
+    for r in range(8):
+        coef = wide_dot(weight_of(r) * entry(2), cover)
+        model[r : r + 1, :] = jnp.sum(pairs[r] * coef, axis=0, keepdims=True)
+    count = wide_dot((upper + lower) * entry(2), cover)
+    scale = 1.0 / jnp.maximum(count, 1.0)
+
     wait_for(recv.at[most], sci_sem.at[1])
 
     def add_block(e, acc):
@@ -323,8 +354,6 @@
             pltpu.VMEM((NPROF, 2 * RW), F32),
             pltpu.VMEM((6 * RW, NPROF * RW), BF16),
             pltpu.VMEM((8, PAIRS, 1024), F32),
-            pltpu.VMEM((8, PAIRS, 1024), BF16),
-            pltpu.VMEM((8, PAIRS, 1024), BF16),
             pltpu.VMEM((32, 8, 256), F32),
             pltpu.VMEM((64, 8, 256), F32),
             pltpu.VMEM((64, 2, 128), F32),

time: 44.3 us -> 40.8 us (0.921)
  Pallas kernels: 40.2 us -> 36.6 us
    pallas_call x1, Pallas kernels: 40.2 us -> 36.6 us  [on_device(): pl.pallas_call(kernel, out_shape=jax.ShapeDtypeStruct((1, 8, 1024), F32),...]
where the time goes in v4:
time: 40.8 us; the launch traced here: 40.6 us
  Pallas kernels  36.6 us (90%)
  between operations  2.59 us (6%)
  local copies, waits for them, and re-layouts  1.38 us (3%)
    pallas_call x1, Pallas kernels, on_device(): pl.pallas_call(kernel, out_shape=jax.ShapeDtypeStruct((1, 8, 1024), F32),...  36.6 us
    unnamed x1, local copies, waits for them, and re-layouts  1.38 us

profile of v4, /device:TPU:1, one launch (start us, length us, event | category | flops | bytes accessed | tf_op | source)
XLA Modules:
  0.0 40.6 jit_solution(12472379054088585106)
XLA Ops:
  2.6 36.6 %difference.1 = f32[1,8,1024]{2,1,0:T(8,128)} custom-call(f32[1,8,1024]{2,1,0:T(8,128)} %coadd.1, f32[1,1,256,256]{3,2,1,0:T(8,128)} %science.1, s32[1,1]{1,0:T(1,128)S(6)} %copy.11.row_offset, s32[1,1]{1,0:T(1,128)S(6)} %copy.12.col_offset, s32[1,1]{1,0:T(1,128)S(6)} %copy.13.intersections, f32[1,1]{1,0:T(1,128)S(6)} %copy.14.visit_weight, ...), custom_call_target="tpu_custom_call" | custom-call | tf_op jit(solution)/shard_map/difference/pallas_call | solution.py:345
  39.2 1.4 %copy.15 = f32[1,8,1024]{2,1,0:T(8,128)} copy(f32[1,8,1024]{2,1,0:T(8,128)} %difference.1) | data formatting | bytes 65536

commit v5 on v4

--- a/solution.py
+++ b/solution.py
@@ -11,6 +11,7 @@
 B = 3
 NPROF = 16
 PAIRS = NPROF * NPROF
+EARLY = 4
 F32 = jnp.float32
 BF16 = jnp.bfloat16
 MESH = pl.DeviceIdType.MESH
@@ -63,12 +64,12 @@
     barrier = pltpu.get_barrier_semaphore()
 
     def greet(k, carry):
-        pl.semaphore_signal(barrier, inc=1, device_id={"epoch": lax.rem(me + k, 64)}, device_id_type=MESH)
+        pl.semaphore_signal(barrier, inc=1, device_id={"epoch": ((me + k) & 63)}, device_id_type=MESH)
         return carry
 
-    lax.fori_loop(1, 64, greet, 0)
+    lax.fori_loop(1, 64, greet, 0, unroll=7)
     for k in (1, 2, 3):
-        pl.semaphore_signal(barrier, inc=1, device_id={"tile": lax.rem(me_t + k, 4)}, device_id_type=MESH)
+        pl.semaphore_signal(barrier, inc=1, device_id={"tile": ((me_t + k) & 3)}, device_id_type=MESH)
 
     for copy in small:
         copy.wait()
@@ -111,15 +112,15 @@
             dst_ref=given.at[me],
             send_sem=par_sem.at[0],
             recv_sem=par_sem.at[1],
-            device_id={"epoch": lax.rem(me + k, 64)},
+            device_id={"epoch": ((me + k) & 63)},
             device_id_type=MESH,
         ).start()
         return carry
 
     def send_science(k, carry):
-        target = lax.rem(me + k, 64)
+        target = ((me + k) & 63)
         pltpu.make_async_remote_copy(
-            src_ref=slots.at[lax.rem(target, 32)],
+            src_ref=slots.at[(target & 31)],
             dst_ref=recv.at[me],
             send_sem=sci_sem.at[0],
             recv_sem=sci_sem.at[1],
@@ -134,16 +135,16 @@
             dst_ref=near.at[2 - d],
             send_sem=halo_send.at[i],
             recv_sem=halo_recv.at[i],
-            device_id={"epoch": lax.rem(me + d + 64, 64)},
+            device_id={"epoch": ((me + d) & 63)},
             device_id_type=MESH,
         )
         for i, d in enumerate((1, -1, 2, -2))
     ]
     for copy in halo:
         copy.start()
-    lax.fori_loop(1, 64, send_params, 0)
-    lax.fori_loop(1, 64, send_science, 0)
-    recv[me] = slots[lax.rem(me, 32)]
+    lax.fori_loop(1, 64, send_params, 0, unroll=7)
+    lax.fori_loop(1, 64, send_science, 0, unroll=7)
+    recv[me] = slots[(me & 31)]
 
     table[...] = jnp.zeros_like(table)
     table[:, 0:KW] = prof[...]
@@ -166,6 +167,8 @@
     down = jnp.dot(
         vertical, near[...].reshape(40, 1024), precision=lax.Precision.HIGHEST, preferred_element_type=F32
     )
+    y_hi, y_lo = split(down)
+    y_all = jnp.concatenate([y_hi, y_lo, y_hi], axis=1)
     def wait_for(ref, sem):
         pltpu.make_async_copy(ref, ref, sem).wait()
 
@@ -195,10 +198,9 @@
                 value = value + jnp.where(block == j - d, taken[:, d * RW : (d + 1) * RW], 0.0)
         spread.append(value)
     g_hi, g_lo = split(jnp.concatenate(spread, axis=1))
-    y_hi, y_lo = split(down)
     caught = lax.dot_general(
         jnp.concatenate([g_hi, g_hi, g_lo], axis=1),
-        jnp.concatenate([y_hi, y_lo, y_hi], axis=1),
+        y_all,
         (((1,), (1,)), ((), ())),
         preferred_element_type=F32,
     )
@@ -221,15 +223,14 @@
             dst_ref=parts.at[me],
             send_sem=lev_sem.at[0],
             recv_sem=lev_sem.at[1],
-            device_id={"epoch": lax.rem(me + k, 64)},
+            device_id={"epoch": ((me + k) & 63)},
             device_id_type=MESH,
         ).start()
         return carry
 
-    lax.fori_loop(1, 64, send_parts, 0)
-
-    down = pltpu.roll(down, HALF, 1)
-    high, low = split(down)
+    lax.fori_loop(1, 64, send_parts, 0, unroll=7)
+
+    high, low = split(pltpu.roll(down, HALF, 1))
 
     def stacked(value):
         def block(j):
@@ -241,7 +242,8 @@
 
     high, low = stacked(high), stacked(low)
     left = jnp.concatenate([high, high, low], axis=1)
-    for step in range(NPROF // 2):
+
+    def make_pairs(step):
         both = jnp.dot(left, hor[:, step * 256 : (step + 1) * 256], preferred_element_type=F32)
         for half in range(2):
             q = 2 * step + half
@@ -252,39 +254,13 @@
                     top = j * 128 + r * NPROF
                     pairs[r, at, cols] = both[top : top + NPROF, half * RW : (half + 1) * RW]
 
+    for step in range(EARLY):
+        make_pairs(step)
+
     across = every.T
 
     def entry(k):
         return across[k : k + 1, :]
-
-    first = every[:, 1:2]
-    column = lax.broadcasted_iota(jnp.int32, (128, 1024), 1).astype(F32)
-    cover = jnp.where((column >= first) & (column < first + float(RW)), 1.0, 0.0).astype(BF16)
-    my_row = (me * 8 + lax.broadcasted_iota(jnp.int32, (8, 128), 0)).astype(F32)
-    inside = my_row - entry(0)
-    upper = jnp.where((inside >= 0.0) & (inside < 128.0), 1.0, 0.0)
-    lower = jnp.where((inside >= 128.0) & (inside < 256.0), 1.0, 0.0)
-
-    pair_id = lax.broadcasted_iota(jnp.int32, (PAIRS, 128), 0).astype(F32)
-    weight = [jnp.zeros((PAIRS, 128), F32)] * 2
-    for b in range(B):
-        same = pair_id == entry(4 + b)
-        weight = [weight[y] + jnp.where(same, entry(7 + 3 * y + b), 0.0) for y in range(2)]
-
-    def weight_of(r):
-        return weight[0] * upper[r : r + 1, :] + weight[1] * lower[r : r + 1, :]
-
-    column = lax.broadcasted_iota(jnp.int32, (8, 1024), 1).astype(F32)
-    rows = (me * 8 + lax.broadcasted_iota(jnp.int32, (8, 1024), 0)).astype(F32)
-
-    def make_mask(e, carry):
-        top = jnp.broadcast_to(given[e, 0:1, 0:1], (8, 1024))
-        side = jnp.broadcast_to(given[e, 0:1, 1:2], (8, 1024))
-        hit = (rows >= top) & (rows < top + 256.0) & (column >= side) & (column < side + 256.0)
-        masks[e] = jnp.where(hit, 1.0, 0.0)
-        return carry
-
-    lax.fori_loop(0, 64, make_mask, 0, unroll=4)
 
     wait_for(parts.at[most], lev_sem.at[1])
     total = jnp.sum(parts[...], axis=0)
@@ -297,13 +273,44 @@
             dst_ref=sums.at[me_t],
             send_sem=sum_send.at[k - 1],
             recv_sem=sum_recv.at[k - 1],
-            device_id={"tile": lax.rem(me_t + k, 4)},
+            device_id={"tile": ((me_t + k) & 3)},
             device_id_type=MESH,
         )
         for k in (1, 2, 3)
     ]
     for copy in sum_copies:
         copy.start()
+
+    first = every[:, 1:2]
+    column = lax.broadcasted_iota(jnp.int32, (128, 1024), 1).astype(F32)
+    cover = jnp.where((column >= first) & (column < first + float(RW)), 1.0, 0.0).astype(BF16)
+    my_row = (me * 8 + lax.broadcasted_iota(jnp.int32, (8, 128), 0)).astype(F32)
+    inside = my_row - entry(0)
+    upper = jnp.where((inside >= 0.0) & (inside < 128.0), 1.0, 0.0)
+    lower = jnp.where((inside >= 128.0) & (inside < 256.0), 1.0, 0.0)
+
+    pair_id = lax.broadcasted_iota(jnp.int32, (PAIRS, 128), 0).astype(F32)
+    weight = [jnp.zeros((PAIRS, 128), F32)] * 2
+    for b in range(B):
+        same = pair_id == entry(4 + b)
+        weight = [weight[y] + jnp.where(same, entry(7 + 3 * y + b), 0.0) for y in range(2)]
+
+    def weight_of(r):
+        return weight[0] * upper[r : r + 1, :] + weight[1] * lower[r : r + 1, :]
+
+    for step in range(EARLY, NPROF // 2):
+        make_pairs(step)
+    column = lax.broadcasted_iota(jnp.int32, (8, 1024), 1).astype(F32)
+    rows = (me * 8 + lax.broadcasted_iota(jnp.int32, (8, 1024), 0)).astype(F32)
+
+    def make_mask(e, carry):
+        top = jnp.broadcast_to(given[e, 0:1, 0:1], (8, 1024))
+        side = jnp.broadcast_to(given[e, 0:1, 1:2], (8, 1024))
+        hit = (rows >= top) & (rows < top + 256.0) & (column >= side) & (column < side + 256.0)
+        masks[e] = jnp.where(hit, 1.0, 0.0)
+        return carry
+
+    lax.fori_loop(0, 64, make_mask, 0, unroll=4)
 
     for r in range(8):
         coef = wide_dot(weight_of(r) * entry(2), cover)

time: 40.8 us -> 41.3 us (1.012)
  Pallas kernels: 36.6 us -> 37.1 us
    pallas_call x1, Pallas kernels: 36.6 us -> 37.1 us  [on_device(): pl.pallas_call(kernel, out_shape=jax.ShapeDtypeStruct((1, 8, 1024), F32),...]
where the time goes in v5:
time: 41.3 us; the launch traced here: 41.1 us
  Pallas kernels  37.1 us (90%)
  between operations  2.59 us (6%)
  local copies, waits for them, and re-layouts  1.38 us (3%)
    pallas_call x1, Pallas kernels, on_device(): pl.pallas_call(kernel, out_shape=jax.ShapeDtypeStruct((1, 8, 1024), F32),...  37.1 us
    unnamed x1, local copies, waits for them, and re-layouts  1.38 us

profile of v5, /device:TPU:1, one launch (start us, length us, event | category | flops | bytes accessed | tf_op | source)
XLA Modules:
  0.0 41.1 jit_solution(15607451022504259186)
XLA Ops:
  2.6 37.1 %difference.1 = f32[1,8,1024]{2,1,0:T(8,128)} custom-call(f32[1,8,1024]{2,1,0:T(8,128)} %coadd.1, f32[1,1,256,256]{3,2,1,0:T(8,128)} %science.1, s32[1,1]{1,0:T(1,128)S(6)} %copy.11.row_offset, s32[1,1]{1,0:T(1,128)S(6)} %copy.12.col_offset, s32[1,1]{1,0:T(1,128)S(6)} %copy.13.intersections, f32[1,1]{1,0:T(1,128)S(6)} %copy.14.visit_weight, ...), custom_call_target="tpu_custom_call" | custom-call | tf_op jit(solution)/shard_map/difference/pallas_call | solution.py:352
  39.7 1.4 %copy.15 = f32[1,8,1024]{2,1,0:T(8,128)} copy(f32[1,8,1024]{2,1,0:T(8,128)} %difference.1) | data formatting | bytes 65536

commit v6 on v5

--- a/solution.py
+++ b/solution.py
@@ -11,6 +11,7 @@
 B = 3
 NPROF = 16
 PAIRS = NPROF * NPROF
+FIRST = 29
 EARLY = 4
 F32 = jnp.float32
 BF16 = jnp.bfloat16
@@ -64,12 +65,12 @@
     barrier = pltpu.get_barrier_semaphore()
 
     def greet(k, carry):
-        pl.semaphore_signal(barrier, inc=1, device_id={"epoch": ((me + k) & 63)}, device_id_type=MESH)
+        pl.semaphore_signal(barrier, inc=1, device_id={"epoch": (me + k) & 63}, device_id_type=MESH)
         return carry
 
     lax.fori_loop(1, 64, greet, 0, unroll=7)
     for k in (1, 2, 3):
-        pl.semaphore_signal(barrier, inc=1, device_id={"tile": ((me_t + k) & 3)}, device_id_type=MESH)
+        pl.semaphore_signal(barrier, inc=1, device_id={"tile": (me_t + k) & 3}, device_id_type=MESH)
 
     for copy in small:
         copy.wait()
@@ -112,13 +113,13 @@
             dst_ref=given.at[me],
             send_sem=par_sem.at[0],
             recv_sem=par_sem.at[1],
-            device_id={"epoch": ((me + k) & 63)},
+            device_id={"epoch": (me + k) & 63},
             device_id_type=MESH,
         ).start()
         return carry
 
     def send_science(k, carry):
-        target = ((me + k) & 63)
+        target = (me + 37 * k) & 63
         pltpu.make_async_remote_copy(
             src_ref=slots.at[(target & 31)],
             dst_ref=recv.at[me],
@@ -135,7 +136,7 @@
             dst_ref=near.at[2 - d],
             send_sem=halo_send.at[i],
             recv_sem=halo_recv.at[i],
-            device_id={"epoch": ((me + d) & 63)},
+            device_id={"epoch": (me + d) & 63},
             device_id_type=MESH,
         )
         for i, d in enumerate((1, -1, 2, -2))
@@ -143,7 +144,7 @@
     for copy in halo:
         copy.start()
     lax.fori_loop(1, 64, send_params, 0, unroll=7)
-    lax.fori_loop(1, 64, send_science, 0, unroll=7)
+    lax.fori_loop(1, FIRST, send_science, 0, unroll=7)
     recv[me] = slots[(me & 31)]
 
     table[...] = jnp.zeros_like(table)
@@ -182,20 +183,20 @@
 
     profile = lax.broadcasted_iota(jnp.int32, (128, NPROF), 1).astype(F32)
     chosen = jnp.concatenate([jnp.where(profile == field(13 + b), 1.0, 0.0) for b in range(B)], axis=0)
-    boxes = jnp.concatenate([jnp.concatenate(box, axis=0), jnp.zeros((NPROF, RW), F32)], axis=1)
-    taken = jnp.dot(chosen, boxes, precision=lax.Precision.HIGHEST, preferred_element_type=F32)
+    taken = jnp.dot(chosen, jnp.concatenate(box, axis=0), precision=lax.Precision.HIGHEST, preferred_element_type=F32)
     start = jnp.broadcast_to((field(1) - float(HALF)).astype(jnp.int32), (128, 128))
     start = jnp.concatenate([start] * B, axis=0)
     turn = jnp.concatenate([start] * 3, axis=1)
     for step in (1, 2, 4, 8, 16, 32, 64):
-        taken = jnp.where((turn & step) != 0, pltpu.roll(taken, step, 1), taken)
+        if step == 64:
+            taken = jnp.concatenate([taken, jnp.zeros((B * 128, RW), F32)], axis=1)
+        taken = jnp.where((turn[:, 0 : taken.shape[1]] & step) != 0, pltpu.roll(taken, step, 1), taken)
     block = start >> 7
     spread = []
     for j in range(8):
-        value = jnp.where(block == j, taken[:, 0:RW], 0.0)
-        for d in (1, 2):
-            if j >= d:
-                value = value + jnp.where(block == j - d, taken[:, d * RW : (d + 1) * RW], 0.0)
+        value = jnp.zeros((B * 128, RW), F32)
+        for d in range(min(j, 2) + 1):
+            value = jnp.where(block == j - d, taken[:, d * RW : (d + 1) * RW], value)
         spread.append(value)
     g_hi, g_lo = split(jnp.concatenate(spread, axis=1))
     caught = lax.dot_general(
@@ -223,12 +224,13 @@
             dst_ref=parts.at[me],
             send_sem=lev_sem.at[0],
             recv_sem=lev_sem.at[1],
-            device_id={"epoch": ((me + k) & 63)},
+            device_id={"epoch": (me + k) & 63},
             device_id_type=MESH,
         ).start()
         return carry
 
     lax.fori_loop(1, 64, send_parts, 0, unroll=7)
+    lax.fori_loop(FIRST, 64, send_science, 0, unroll=7)
 
     high, low = split(pltpu.roll(down, HALF, 1))
 
@@ -273,7 +275,7 @@
             dst_ref=sums.at[me_t],
             send_sem=sum_send.at[k - 1],
             recv_sem=sum_recv.at[k - 1],
-            device_id={"tile": ((me_t + k) & 3)},
+            device_id={"tile": (me_t + k) & 3},
             device_id_type=MESH,
         )
         for k in (1, 2, 3)

time: 41.3 us -> 39.4 us (0.954)
  Pallas kernels: 37.1 us -> 35.2 us
    pallas_call x1, Pallas kernels: 37.1 us -> 35.2 us  [on_device(): pl.pallas_call(kernel, out_shape=jax.ShapeDtypeStruct((1, 8, 1024), F32),...]
where the time goes in v6:
time: 39.4 us; the launch traced here: 39.2 us
  Pallas kernels  35.2 us (89%)
  between operations  2.59 us (7%)
  local copies, waits for them, and re-layouts  1.38 us (4%)
    pallas_call x1, Pallas kernels, on_device(): pl.pallas_call(kernel, out_shape=jax.ShapeDtypeStruct((1, 8, 1024), F32),...  35.2 us
    unnamed x1, local copies, waits for them, and re-layouts  1.38 us

profile of v6, /device:TPU:1, one launch (start us, length us, event | category | flops | bytes accessed | tf_op | source)
XLA Modules:
  0.0 39.2 jit_solution(15999029661136621171)
XLA Ops:
  2.6 35.2 %difference.1 = f32[1,8,1024]{2,1,0:T(8,128)} custom-call(f32[1,8,1024]{2,1,0:T(8,128)} %coadd.1, f32[1,1,256,256]{3,2,1,0:T(8,128)} %science.1, s32[1,1]{1,0:T(1,128)S(6)} %copy.11.row_offset, s32[1,1]{1,0:T(1,128)S(6)} %copy.12.col_offset, s32[1,1]{1,0:T(1,128)S(6)} %copy.13.intersections, f32[1,1]{1,0:T(1,128)S(6)} %copy.14.visit_weight, ...), custom_call_target="tpu_custom_call" | custom-call | tf_op jit(solution)/shard_map/difference/pallas_call | solution.py:354
  37.8 1.4 %copy.15 = f32[1,8,1024]{2,1,0:T(8,128)} copy(f32[1,8,1024]{2,1,0:T(8,128)} %difference.1) | data formatting | bytes 65536

commit v7 on v6

--- a/solution.py
+++ b/solution.py
@@ -100,10 +100,6 @@
         row = jnp.where(lane == k, entry, row)
     given[me] = row
 
-    sci_copy.wait()
-    image = sci[...]
-    science_sum = jnp.sum(image)
-    slots[...] = (roll_by(roll_by(image, ox & 255, 1), oy & 255, 0) * gain).reshape(32, 8, 256)
     own_copy.wait()
     pl.semaphore_wait(barrier, 66)
 
@@ -144,6 +140,11 @@
     for copy in halo:
         copy.start()
     lax.fori_loop(1, 64, send_params, 0, unroll=7)
+
+    sci_copy.wait()
+    image = sci[...]
+    science_sum = jnp.sum(image)
+    slots[...] = (roll_by(roll_by(image, ox & 255, 1), oy & 255, 0) * gain).reshape(32, 8, 256)
     lax.fori_loop(1, FIRST, send_science, 0, unroll=7)
     recv[me] = slots[(me & 31)]
 

time: 39.4 us -> 39.4 us (level)
  no operation moved by 1% of the time
where the time goes in v7:
time: 39.4 us; the launch traced here: 39.2 us
  Pallas kernels  35.2 us (89%)
  between operations  2.59 us (7%)
  local copies, waits for them, and re-layouts  1.38 us (4%)
    pallas_call x1, Pallas kernels, on_device(): pl.pallas_call(kernel, out_shape=jax.ShapeDtypeStruct((1, 8, 1024), F32),...  35.2 us
    unnamed x1, local copies, waits for them, and re-layouts  1.38 us

profile of v7, /device:TPU:1, one launch (start us, length us, event | category | flops | bytes accessed | tf_op | source)
XLA Modules:
  0.0 39.2 jit_solution(11519487828201318027)
XLA Ops:
  2.6 35.2 %difference.1 = f32[1,8,1024]{2,1,0:T(8,128)} custom-call(f32[1,8,1024]{2,1,0:T(8,128)} %coadd.1, f32[1,1,256,256]{3,2,1,0:T(8,128)} %science.1, s32[1,1]{1,0:T(1,128)S(6)} %copy.11.row_offset, s32[1,1]{1,0:T(1,128)S(6)} %copy.12.col_offset, s32[1,1]{1,0:T(1,128)S(6)} %copy.13.intersections, f32[1,1]{1,0:T(1,128)S(6)} %copy.14.visit_weight, ...), custom_call_target="tpu_custom_call" | custom-call | tf_op jit(solution)/shard_map/difference/pallas_call | solution.py:355
  37.8 1.4 %copy.15 = f32[1,8,1024]{2,1,0:T(8,128)} copy(f32[1,8,1024]{2,1,0:T(8,128)} %difference.1) | data formatting | bytes 65536
